TPU v7x, 256 devices: a whole 4x4x8 slice. The times are simulated.
256 devices in a mesh: dp: 32 (over x, z), expert: 8 (over y, core).
Axes of the slice: x: 4, y: 4, z: 8, core: 2. Of those that a mesh axis runs over, the one named last changes fastest.
Arguments:
- tokens: bfloat16 [3072, 3072], P(('dp', 'expert')), may hold values from -6 to 6
- cotangent: bfloat16 [3072, 3072], P(('dp', 'expert')), may hold values from -6 to 6
- routes: int32 [3072, 2], P(('dp', 'expert')), may hold values from 0 to 7, all different within a row; in each aligned block of 12 rows (0 to 11, 12 to 23, ...) at most 4 rows name the same one
- example_ids: int32 [32, 96], P('dp', 'expert'), may hold values from 0 to 5, never falling along the last dimension, each value on 1 to 32 neighbouring positions
- w_gate: bfloat16 [8, 3072, 8192], P('expert', None, 'dp'), may hold values from -0.109375 to 0.109375
- w_up: bfloat16 [8, 3072, 8192], P('expert', None, 'dp'), may hold values from -0.109375 to 0.109375
- w_down: bfloat16 [8, 8192, 3072], P('expert', 'dp'), may hold values from -0.0625 to 0.0625
Outputs:
- mixed: bfloat16 [3072, 3072], P(('dp', 'expert'))
- example_norms: float32 [32, 6], P('dp')
- grad_gate: bfloat16 [8, 3072, 8192], P('expert', None, 'dp')
- grad_up: bfloat16 [8, 3072, 8192], P('expert', None, 'dp')
- grad_down: bfloat16 [8, 8192, 3072], P('expert', 'dp')
Inputs may be any that keep to these rules, and one draw needn't show every extreme that they name: `routes`: among the tokens of one device each expert is named at most 4 times, and exactly 4 times by some expert. `example_ids`: along a row example numbers never fall and every example has at least one token.
All inputs are finite; a program needn't handle non-finite values.
Results may differ from a plain program's by a relative error of at most 0.0059.
Values may be sent and summed in bfloat16 or wider, within the bound.
No kernel may reach another device: no remote copies, remote signals or barrier semaphores. Data moves between devices by JAX's collectives and lax.ppermute only.
A program may use at most 128 MiB of HBM per device.

v0:
```python
import math

import jax
import jax.numpy as jnp
from jax import lax
from jax.sharding import PartitionSpec as P

D = 3072
FF = 8192
CAP = 4
EX_ROW = 6


GAMMA = 0.01


def blocked_gram(blocked):
    return jnp.einsum("bid,bjd->bij", blocked, blocked, preferred_element_type=jnp.float32)


def on_device(tokens, cotangent, routes, example_ids, w_gate, w_up, w_down):
    n_data = lax.axis_size("dp")
    n_owner = lax.axis_size("expert")
    my_row = lax.axis_index("dp")
    tok_count = tokens.shape[0]
    width = tokens.shape[1]
    slots = n_owner * CAP
    ex_total = n_data * EX_ROW
    radius = math.sqrt(3.0 * D * FF * n_owner / ex_total)
    global_ids = example_ids.reshape(-1) + my_row * EX_ROW
    flat_routes = routes.reshape(-1)
    owner_hot = (flat_routes[:, None] == jnp.arange(n_owner)[None, :]).astype(jnp.int32)
    before = jnp.cumsum(owner_hot, axis=0) - owner_hot
    slot_of = flat_routes * CAP + jnp.sum(before * owner_hot, axis=1)
    placed = (jnp.arange(slots)[:, None] == slot_of[None, :]).astype(jnp.int32)
    placed = jnp.sum(placed.reshape(slots, tok_count, 2), axis=2)
    placed_bf = placed.astype(jnp.bfloat16)
    filled = jnp.sum(placed, axis=1) > 0
    send_ids = jnp.where(filled, jnp.sum(placed * global_ids[None, :], axis=1), -1)
    send_x = jnp.dot(placed_bf, tokens, preferred_element_type=jnp.float32).astype(jnp.bfloat16)
    send_dy = jnp.dot(placed_bf, cotangent, preferred_element_type=jnp.float32).astype(jnp.bfloat16)
    recv_x, recv_dy, recv_ids = (
        lax.all_to_all(
            send_x.reshape(n_owner, CAP, width), "expert", split_axis=0, concat_axis=0, tiled=True
        ),
        lax.all_to_all(
            send_dy.reshape(n_owner, CAP, width), "expert", split_axis=0, concat_axis=0, tiled=True
        ),
        lax.all_to_all(
            send_ids.reshape(n_owner, CAP), "expert", split_axis=0, concat_axis=0, tiled=True
        ),
    )
    local_x = recv_x.reshape(slots, width)
    local_dy = recv_dy.reshape(slots, width)
    local_ids = recv_ids.reshape(slots)
    rows_x, rows_dy, rows_ids = (
        lax.all_gather(local_x, "dp", axis=0, tiled=True),
        lax.all_gather(local_dy, "dp", axis=0, tiled=True),
        lax.all_gather(local_ids, "dp", axis=0, tiled=True),
    )
    gate = jnp.dot(rows_x, w_gate[0], preferred_element_type=jnp.float32)
    up = jnp.dot(rows_x, w_up[0], preferred_element_type=jnp.float32)
    sig = jax.nn.sigmoid(gate)
    swish = gate * sig
    hidden = (swish * up).astype(jnp.bfloat16)
    own_out = lax.psum_scatter(
        jnp.dot(hidden, w_down[0], preferred_element_type=jnp.float32),
        "dp",
        scatter_dimension=0,
        tiled=True,
    ).astype(jnp.bfloat16)
    returned = lax.all_to_all(
        own_out.reshape(n_owner, CAP, width), "expert", split_axis=0, concat_axis=0, tiled=True
    )
    mixed = jnp.dot(
        placed_bf.T, returned.reshape(slots, width), preferred_element_type=jnp.float32
    ).astype(jnp.bfloat16)
    back_hidden = lax.dot_general(
        rows_dy, w_down[0], (((1,), (1,)), ((), ())), preferred_element_type=jnp.float32
    )
    d_gate = (back_hidden * up * sig * (1.0 + gate * (1.0 - sig))).astype(jnp.bfloat16)
    d_up = (back_hidden * swish).astype(jnp.bfloat16)
    hidden_width = hidden.shape[1]
    pair_value = blocked_gram(rows_x.reshape(n_data, slots, width)) * (
        blocked_gram(d_gate.reshape(n_data, slots, hidden_width))
        + blocked_gram(d_up.reshape(n_data, slots, hidden_width))
    )
    pair_value = pair_value + blocked_gram(
        hidden.reshape(n_data, slots, hidden_width)
    ) * blocked_gram(rows_dy.reshape(n_data, slots, width))
    id_blocks = rows_ids.reshape(n_data, slots)
    same = (id_blocks[:, :, None] == id_blocks[:, None, :]) & (id_blocks[:, :, None] >= 0)
    row_sums = jnp.sum(jnp.where(same, pair_value, 0.0), axis=2).reshape(-1)
    ex_hot = (rows_ids[:, None] == jnp.arange(ex_total)[None, :]).astype(jnp.float32)
    partial_value = jnp.sum(ex_hot * row_sums[:, None], axis=0)
    squares = lax.psum(partial_value, ("dp", "expert"))
    norms_all = jnp.sqrt(squares)
    factors = radius / (norms_all + GAMMA)
    own_norms = lax.dynamic_slice_in_dim(norms_all, my_row * EX_ROW, EX_ROW, 0)
    row_factor = jnp.sum(ex_hot * factors[None, :], axis=1)[:, None]
    gate_scaled = (row_factor * d_gate).astype(jnp.bfloat16)
    up_scaled = (row_factor * d_up).astype(jnp.bfloat16)
    cot_scaled = (row_factor * rows_dy).astype(jnp.bfloat16)
    over_rows = (((0,), (0,)), ((), ()))
    grad_gate = lax.dot_general(
        rows_x, gate_scaled, over_rows, preferred_element_type=jnp.float32
    ).astype(jnp.bfloat16)
    grad_up = lax.dot_general(
        rows_x, up_scaled, over_rows, preferred_element_type=jnp.float32
    ).astype(jnp.bfloat16)
    grad_down = lax.dot_general(
        hidden, cot_scaled, over_rows, preferred_element_type=jnp.float32
    ).astype(jnp.bfloat16)
    return (mixed, own_norms.reshape(1, EX_ROW), grad_gate[None], grad_up[None], grad_down[None])


def solution(mesh):
    placed = (
        P(("dp", "expert"), None),
        P(("dp", "expert"), None),
        P(("dp", "expert"), None),
        P("dp", "expert"),
        P("expert", None, "dp"),
        P("expert", None, "dp"),
        P("expert", "dp", None),
    )
    return jax.shard_map(
        on_device,
        mesh=mesh,
        in_specs=placed,
        out_specs=(
            P(("dp", "expert"), None),
            P("dp", None),
            P("expert", None, "dp"),
            P("expert", None, "dp"),
            P("expert", "dp", None),
        ),
        check_vma=False,
    )
```

profile of v0, /device:TPU:1, one launch (start us, length us, event | category | flops | bytes accessed | tf_op | source)
XLA Modules:
  0.0 469.0 jit_solution(9517063691811172024)
XLA Ops:
  7.2 0.0 copy-start
  7.2 0.0 all-gather.3.cloned.1.call-start
  7.2 0.9 copy.26
  8.1 0.1 eq.58
  8.2 0.1 fusion.21
  8.3 0.2 select_reduce_fusion.2
  8.5 0.1 reduce_sum.66
  8.6 0.1 copy.27
  8.7 0.7 multiply_add_fusion
  9.4 0.1 copy.28
  9.5 0.1 fusion.22
  9.6 1.1 convolution_convert_fusion.3
  10.7 0.1 reshape.112
  10.8 11.7 %all_to_all.21 = bf16[8,4,3072]{2,1,0:T(4,128)(2,1)S(1)} all-to-all(bf16[8,4,3072]{2,1,0:T(4,128)(2,1)S(1)} %reshape.112), channel_id=1, replica_groups=mesh['dp'=32,'expert'=8] {'expert'}, dimensions={0} | all-to-all | bytes 393216 | tf_op jit(solution)/shard_map/all_to_all | solution.py:43
  22.4 0.7 reshape.113
  23.2 0.0 all-gather.3.cloned.1.call-update
  23.2 0.0 all-gather.5.cloned.1.call-start
  23.2 1.1 convolution_convert_fusion.2
  24.4 0.1 reshape.118
  24.5 9.2 %all_to_all.22 = bf16[8,4,3072]{2,1,0:T(4,128)(2,1)S(1)} all-to-all(bf16[8,4,3072]{2,1,0:T(4,128)(2,1)S(1)} %reshape.118), channel_id=1, replica_groups=mesh['dp'=32,'expert'=8] {'expert'}, dimensions={0} | all-to-all | bytes 393216 | tf_op jit(solution)/shard_map/all_to_all | solution.py:46
  33.7 0.7 reshape.119
  34.4 0.0 all-gather.5.cloned.1.call-update
  34.5 0.0 reduce-scatter.2.cloned.1.call-start
  34.5 78.4 %all-gather.3.cloned.1.call-done = bf16[1024,3072]{1,0:T(8,128)(2,1)} async-done(((bf16[32,3072]{1,0:T(8,128)(2,1)}), bf16[1024,3072]{1,0:T(8,128)(2,1)}) %all-gather.3.cloned.1.call-update) | async-done | bytes 6291472 | tf_op jit(solution)/shard_map/all_gather | solution.py:57
  112.9 6.1 %fusion.10 = f32[1024,256]{1,0:T(8,128)} fusion(bf16[1024,3072]{1,0:T(8,128)(2,1)} %all-gather.3.cloned.1.call-done, bf16[1,3072,256]{2,1,0:T(8,128)(2,1)} %param.12), kind=kOutput, calls=%fused_computation.16 | convolution fusion | flops 1610612736 | bytes 8912896 | tf_op jit(solution)/shard_map/dot_general | solution.py:62
  119.0 4.2 fusion.12
  123.2 78.5 %all-gather.5.cloned.1.call-done = bf16[1024,3072]{1,0:T(8,128)(2,1)} async-done(((bf16[32,3072]{1,0:T(8,128)(2,1)}), bf16[1024,3072]{1,0:T(8,128)(2,1)}) %all-gather.5.cloned.1.call-update) | async-done | bytes 6291472 | tf_op jit(solution)/shard_map/all_gather | solution.py:58
  201.7 0.0 copy-done
  201.7 5.5 %multiply_convert_fusion.8 = (bf16[1024,256]{1,0:T(8,128)(2,1)S(1)}, bf16[1024,256]{1,0:T(8,128)(2,1)S(1)}, bf16[1024,256]{1,0:T(8,128)(2,1)S(1)}) fusion(f32[1024,256]{1,0:T(8,128)} %fusion.12, f32[1024,256]{1,0:T(8,128)} %fusion.10, bf16[1024,3072]{1,0:T(8,128)(2,1)} %all-gather.5.cloned.1.call-done, bf16[1,256,3072]{2,1,0:T(8,128)(2,1)S(1)} %copy-done), kind=kOutput, calls=%fused_computation.28 | convolution fusion | flops 1614544896 | bytes 11534336 | tf_op jit(solution)/shard_map/dot_general | solution.py:78
  207.2 6.4 %fusion.8 = f32[1024,3072]{1,0:T(8,128)} fusion(bf16[1024,256]{1,0:T(8,128)(2,1)S(1)} %get-tuple-element.9, bf16[1,256,3072]{2,1,0:T(8,128)(2,1)S(1)} %copy-done), kind=kOutput, calls=%fused_computation.14 | convolution fusion | flops 1610612736 | bytes 14680064 | tf_op jit(solution)/shard_map/dot_general | solution.py:67
  213.6 0.0 reduce-scatter.2.cloned.1.call-update
  213.6 0.6 copy-done.2
  214.2 0.1 multiply_reduce_fusion
  214.3 0.7 select_n.23
  215.0 5.3 %all-to-all-start.2 = ((s32[8,1,4]{2,1,0:T(1,128)}), s32[8,1,4]{2,1,0:T(1,128)S(1)}, u32[]{:S(2)}, u32[]{:S(2)}) async-start(s32[8,1,4]{2,1,0:T(1,128)} %bitcast.4), calls=%async_computation.3 | async-start | bytes 8192 | tf_op jit(solution)/shard_map/all_to_all | solution.py:49
  220.3 0.6 dynamic-slice
  221.6 3.3 all-to-all-done.2
  224.8 0.5 broadcast.69
  225.3 0.7 reduce.4
  226.0 0.1 reshape.125
  226.1 0.2 dynamic-update-slice
  226.3 13.8 %all-reduce = s32[1024]{0:T(1024)S(1)} all-reduce(s32[1024]{0:T(1024)S(1)} %dynamic-update-slice), channel_id=1, replica_groups=mesh['dp'=32,'expert'=8] {'dp'}, use_global_device_ids=true, to_apply=%add | all-reduce | flops 1024 | bytes 8192
  240.1 0.1 eq.67
  240.2 0.3 fusion.28
  240.4 0.0 slice-start.1
  240.4 6.6 %fusion.27 = f32[32,32,32]{1,2,0:T(8,128)S(1)} fusion(bf16[32,32,3072]{2,1,0:T(8,128)(2,1)} %bitcast.53), kind=kOutput, calls=%fused_computation.54 | convolution fusion | flops 201326592 | bytes 6422528 | tf_op jit(solution)/shard_map/bid,bjd->bij/dot_general | solution.py:18
  247.1 0.3 fusion.16
  247.4 0.0 slice-done
  247.4 1.8 fusion.29
  249.2 0.4 fusion.17
  249.6 0.1 mul.106
  249.6 0.2 select_reduce_fusion.1
  249.8 78.8 %psum.7 = f32[192]{0:T(256)S(1)} all-reduce(f32[192]{0:T(256)S(1)} %select_reduce_fusion.1), channel_id=1, replica_groups=mesh['dp'=32,'expert'=8] {'dp','expert'}, use_global_device_ids=true, to_apply=%region_8.9 | all-reduce | flops 192 | bytes 1536 | tf_op jit(solution)/shard_map/psum | solution.py:96
  328.6 0.2 select_reduce_fusion
  328.8 6.0 %fusion.5 = bf16[1,3072,256]{2,1,0:T(8,128)(2,1)} fusion(bf16[1024,3072]{1,0:T(8,128)(2,1)} %all-gather.3.cloned.1.call-done, bf16[1024,256]{1,0:T(8,128)(2,1)S(1)} %get-tuple-element.7, f32[1024]{0:T(1024)S(1)} %select_reduce_fusion), kind=kOutput, calls=%fused_computation.8 | convolution fusion | flops 1612185600 | bytes 8392704 | tf_op jit(solution)/shard_map/dot_general | solution.py:108
  334.8 6.1 %fusion.4 = bf16[1,3072,256]{2,1,0:T(8,128)(2,1)} fusion(bf16[1024,3072]{1,0:T(8,128)(2,1)} %all-gather.3.cloned.1.call-done, bf16[1024,256]{1,0:T(8,128)(2,1)S(1)} %get-tuple-element.8, f32[1024]{0:T(1024)S(1)} %select_reduce_fusion), kind=kOutput, calls=%fused_computation.7 | convolution fusion | flops 1612185600 | bytes 8392704 | tf_op jit(solution)/shard_map/dot_general | solution.py:105
  340.9 103.5 %reduce-scatter.2.cloned.1.call-done = f32[32,3072]{1,0:T(8,128)} async-done(((f32[1024,3072]{1,0:T(8,128)}), f32[32,3072]{1,0:T(8,128)}) %reduce-scatter.2.cloned.1.call-update) | async-done | bytes 393232 | tf_op jit(solution)/shard_map/reduce_scatter | solution.py:66
  444.3 1.0 convert_element_type.64
  445.4 0.8 reshape.114
  446.1 9.0 %all-to-all-start.1 = ((bf16[8,4,3072]{2,1,0:T(4,128)(2,1)}), bf16[8,4,3072]{2,1,0:T(4,128)(2,1)S(1)}, u32[]{:S(2)}, u32[]{:S(2)}) async-start(bf16[8,4,3072]{2,1,0:T(4,128)(2,1)} %reshape.114), calls=%async_computation.2 | async-start | bytes 393216 | tf_op jit(solution)/shard_map/all_to_all | solution.py:72
  455.1 6.0 %fusion.3 = bf16[1,256,3072]{2,1,0:T(8,128)(2,1)} fusion(bf16[1024,256]{1,0:T(8,128)(2,1)S(1)} %get-tuple-element.9, bf16[1024,3072]{1,0:T(8,128)(2,1)} %all-gather.5.cloned.1.call-done, f32[1024]{0:T(1024)S(1)} %select_reduce_fusion), kind=kOutput, calls=%fused_computation.6 | convolution fusion | flops 1620836352 | bytes 8392704 | tf_op jit(solution)/shard_map/dot_general | solution.py:111
  461.1 0.6 dynamic-slice_bitcast_fusion
  461.7 0.0 all-to-all-done.1
  461.7 0.8 convolution_convert_fusion.4
  (15 shorter events, 0.1 us)
Async XLA Ops:
  7.2 194.6 %copy-start = (bf16[1,256,3072]{2,1,0:T(8,128)(2,1)S(1)}, bf16[1,256,3072]{2,1,0:T(8,128)(2,1)}, u32[]{:S(2)}) copy-start(bf16[1,256,3072]{2,1,0:T(8,128)(2,1)} %param.13) | copy-start | bytes 4718596
  7.2 105.7 %all-gather.3.cloned.1.call-start = ((), (), s32[]{:S(2)}) async-start(), calls=%async_computation.5 | async-start | bytes 6488064 | tf_op jit(solution)/shard_map/all_gather | solution.py:57
  23.2 178.5 %all-gather.5.cloned.1.call-start = ((), (), s32[]{:S(2)}) async-start(), calls=%async_computation.7 | async-start | bytes 6488064 | tf_op jit(solution)/shard_map/all_gather | solution.py:58
  34.5 409.9 %reduce-scatter.2.cloned.1.call-start = ((), (), s32[]{:S(2)}) async-start(), calls=%async_computation.6 | async-start | bytes 12976128 | tf_op jit(solution)/shard_map/reduce_scatter | solution.py:66
  112.9 6.1 %copy-start.1 = (bf16[1024,3072]{1,0:T(8,128)(2,1)S(1)}, bf16[1024,3072]{1,0:T(8,128)(2,1)}, u32[]{:S(2)}) copy-start(bf16[1024,3072]{1,0:T(8,128)(2,1)} %all-gather.3.cloned.1.call-done) | copy-start | bytes 18874372
  213.6 0.7 copy-start.2
  213.6 6.8 %copy-start.3 = (u32[256]{0:T(256)S(1)}, u32[256]{0:T(256)}, u32[]{:S(2)}) copy-start(u32[256]{0:T(256)} %constant.41) | copy-start | bytes 3076
  215.0 9.8 %all-to-all-start.2 = ((s32[8,1,4]{2,1,0:T(1,128)}), s32[8,1,4]{2,1,0:T(1,128)S(1)}, u32[]{:S(2)}, u32[]{:S(2)}) async-start(s32[8,1,4]{2,1,0:T(1,128)} %bitcast.4), calls=%async_computation.3 | async-start | bytes 8192 | tf_op jit(solution)/shard_map/all_to_all | solution.py:49
  240.2 7.2 %slice-start = ((s8[6291456]{0:T(1024)(128)(4,1)}), s8[4194304]{0:T(1024)(128)(4,1)S(1)}, s32[]{:S(2)}) async-start(s8[6291456]{0:T(1024)(128)(4,1)} %bitcast.54), calls=%async_computation.8 | async-start | bytes 8388608
  240.4 7.0 %slice-start.1 = ((s8[6291456]{0:T(1024)(128)(4,1)}), s8[2097152]{0:T(1024)(128)(4,1)S(1)}, s32[]{:S(2)}) async-start(s8[6291456]{0:T(1024)(128)(4,1)} %bitcast.54), calls=%async_computation.9 | async-start | bytes 4194304
  446.1 15.6 %all-to-all-start.1 = ((bf16[8,4,3072]{2,1,0:T(4,128)(2,1)}), bf16[8,4,3072]{2,1,0:T(4,128)(2,1)S(1)}, u32[]{:S(2)}, u32[]{:S(2)}) async-start(bf16[8,4,3072]{2,1,0:T(4,128)(2,1)} %reshape.114), calls=%async_computation.2 | async-start | bytes 393216 | tf_op jit(solution)/shard_map/all_to_all | solution.py:72
Sparse Core Ops, SparseCore 0:
  23.3 89.5 all-gather.2
  116.0 85.6 all-gather.4
  213.7 230.5 reduce-scatter.1
where the time goes:
time: 470 us; the launch traced here: 469 us
  waiting for transfers between devices  264 us (56%)
  blocking collectives  113 us (24%)
  matrix products  52.5 us (11%)
  between operations  14.5 us (3%)
  starting transfers between devices  14.4 us (3%)
  local copies, waits for them, and re-layouts  7.09 us (2%)
    reduce_scatter x1, waiting for transfers between devices, on_device(): lax.psum_scatter(jnp.dot(hidden, w_down[0], preferred_element_type=jnp.fl...  103 us
    psum x1, blocking collectives, on_device(): squares = lax.psum(partial_value, ('dp', 'expert'))  78.8 us
    all_gather x1, waiting for transfers between devices, on_device(): lax.all_gather(local_dy, 'dp', axis=0, tiled=True)  78.5 us
    all_gather x1, waiting for transfers between devices, on_device(): lax.all_gather(local_x, 'dp', axis=0, tiled=True)  78.4 us
    unnamed x1, blocking collectives  13.8 us
    all_to_all x1, blocking collectives, on_device(): lax.all_to_all(send_x.reshape(n_owner, CAP, width), 'expert', split_axis=...  11.7 us
  transfers between devices with their start and end apart: 5, of which 4 were waited for; matrix products, arithmetic and copies ran while one was open for 9% of the time, Pallas kernels for 0%

commit v1 on v0

v1 whole, which is shorter than its diff:
```python
import math

import jax
import jax.numpy as jnp
from jax import lax
from jax.experimental import pallas as pl
from jax.experimental.pallas import tpu as pltpu
from jax.sharding import Mesh, PartitionSpec as P

D = 3072
FF = 8192
CAP = 4
EX_ROW = 6
NX, NZ, NE = 4, 8, 8
BLOCKS = NX * NZ
SLOTS = NE * CAP
ROWS = BLOCKS * SLOTS
HID = FF // BLOCKS
SIZE = {"x": NX, "z": NZ}
GAMMA = 0.01
EXPERT = ("y", "c")
BF = jnp.bfloat16
F32 = jnp.float32
MIB = 1 << 20
PER = 8
TILE = PER * SLOTS
COLS = 512


def shift(a, axis, step):
    n = SIZE[axis]
    return lax.ppermute(a, axis, [(i, (i + step) % n) for i in range(n)])


def plus(a, b):
    return (a.astype(F32) + b.astype(F32)).astype(BF)


def ring_sum(get, axis, mid):
    half = SIZE[axis] // 2
    far = get(half)
    up, down = shift(far[..., :mid, :], axis, 1), shift(far[..., mid:, :], axis, -1)
    own_up, own_down = get(half - 1), get(1 - half)
    up = jnp.concatenate([plus(up, own_up[..., :mid, :]), own_up[..., mid:, :]], axis=-2)
    down = jnp.concatenate([own_down[..., :mid, :], plus(down, own_down[..., mid:, :])], axis=-2)
    for k in range(half - 1, 0, -1):
        up, down = shift(up, axis, 1), shift(down, axis, -1)
        if k > 1:
            up, down = plus(up, get(k - 1)), plus(down, get(1 - k))
    return (up.astype(F32) + down.astype(F32) + get(0).astype(F32)).astype(BF)


def direct_sum(get, axis):
    n = SIZE[axis]
    total = get(0).astype(F32)
    for k in range(1, n):
        total = total + shift(get(k), axis, k).astype(F32)
    return total.astype(BF)


def sum_z_x(part, ix, iz):
    part = part.reshape(NX, NZ, SLOTS, -1)
    w = part.shape[-1]
    line = ring_sum(lambda k: lax.dynamic_slice(part, (0, (iz + k) % NZ, 0, 0), (NX, 1, SLOTS, w)), "z", SLOTS // 2)
    return direct_sum(lambda k: lax.dynamic_slice(line, ((ix + k) % NX, 0, 0, 0), (1, 1, SLOTS, w)), "x")[0, 0]


def sum_x_z(part, ix, iz):
    part = part.reshape(NX, NZ, SLOTS, -1)
    w = part.shape[-1]
    line = ring_sum(lambda k: lax.dynamic_slice(part, ((ix + k) % NX, 0, 0, 0), (1, NZ, SLOTS, w)), "x", SLOTS // 2)
    return direct_sum(lambda k: lax.dynamic_slice(line, (0, (iz + k) % NZ, 0, 0), (1, 1, SLOTS, w)), "z")[0, 0]


def spread(a, axes, n):
    return lax.all_to_all(jnp.broadcast_to(a[None], (n,) + a.shape), axes, 0, 0, tiled=True)


def dot(a, b, dims):
    return lax.dot_general(a, b, (dims, ((), ())), preferred_element_type=F32)


def forward_kernel(x_ref, wg_ref, wu_ref, wd_ref, gate_ref, up_ref, hidden_ref, left_ref, right_ref):
    x = x_ref[...].reshape(TILE, D)
    gate = dot(x, wg_ref[0], ((1,), (0,)))
    up = dot(x, wu_ref[0], ((1,), (0,)))
    hidden = (gate * jax.nn.sigmoid(gate) * up).astype(BF)
    gate_ref[...] = gate
    up_ref[...] = up
    hidden_ref[...] = hidden
    w = left_ref.shape[1]
    left_ref[...] = dot(hidden, wd_ref[0, :, :w], ((1,), (0,))).astype(BF)
    right_ref[...] = dot(hidden, wd_ref[0, :, w:], ((1,), (0,))).astype(BF)


def forward(both, w_gate, w_up, w_down, w):
    def whole(a):
        return pl.BlockSpec(a.shape, lambda i: (0, 0, 0), pipeline_mode=pl.Buffered(1))

    def tall(n):
        return pl.BlockSpec((TILE, n), lambda i: (i, 0))

    return pl.pallas_call(
        forward_kernel,
        grid=(BLOCKS // PER,),
        in_specs=[pl.BlockSpec((PER, SLOTS, D), lambda i: (i, 0, 0)), whole(w_gate), whole(w_up), whole(w_down)],
        out_specs=[tall(HID), tall(HID), tall(HID), tall(w), tall(D - w)],
        out_shape=[
            jax.ShapeDtypeStruct((ROWS, HID), F32),
            jax.ShapeDtypeStruct((ROWS, HID), F32),
            jax.ShapeDtypeStruct((ROWS, HID), BF),
            jax.ShapeDtypeStruct((ROWS, w), BF),
            jax.ShapeDtypeStruct((ROWS, D - w), BF),
        ],
        compiler_params=pltpu.CompilerParams(vmem_limit_bytes=40 * MIB),
        cost_estimate=pl.CostEstimate(flops=6 * ROWS * D * HID, bytes_accessed=20 * MIB, transcendentals=ROWS * HID),
        name="forward",
    )(both, w_gate, w_up, w_down)


def backward_kernel(y_ref, wd_ref, gate_ref, up_ref, hidden_ref, xx_ref, yy_ref, id_col_ref, id_row_ref, dg_ref, du_ref, sum_ref):
    back = dot(y_ref[...].reshape(TILE, D), wd_ref[0], ((1,), (1,)))
    gate, up, hidden = gate_ref[...], up_ref[...], hidden_ref[...]
    sig = jax.nn.sigmoid(gate)
    d_gate = (back * up * sig * (1.0 + gate * (1.0 - sig))).astype(BF)
    d_up = (back * (gate * sig)).astype(BF)
    dg_ref[...] = d_gate
    du_ref[...] = d_up
    last = ((1,), (1,))
    xx = jnp.concatenate([xx_ref[...]] * PER, axis=1)
    yy = jnp.concatenate([yy_ref[...]] * PER, axis=1)
    pair = xx * (dot(d_gate, d_gate, last) + dot(d_up, d_up, last)) + yy * dot(hidden, hidden, last)
    block_row = lax.broadcasted_iota(jnp.int32, (TILE, TILE), 0) // SLOTS
    block_col = lax.broadcasted_iota(jnp.int32, (TILE, TILE), 1) // SLOTS
    ids_col, ids_row = id_col_ref[...], id_row_ref[0]
    same = (block_row == block_col) & (ids_col == ids_row) & (ids_col >= 0.0)
    sum_ref[...] = jnp.sum(jnp.where(same, pair, 0.0), axis=1, keepdims=True)


def backward(both, w_down, gate, up, hidden, xx, yy, ids):
    def tall(n):
        return pl.BlockSpec((TILE, n), lambda i: (i, 0))

    steps = BLOCKS // PER
    return pl.pallas_call(
        backward_kernel,
        grid=(steps,),
        in_specs=[
            pl.BlockSpec((PER, SLOTS, D), lambda i: (i, 1, 0)),
            pl.BlockSpec(w_down.shape, lambda i: (0, 0, 0), pipeline_mode=pl.Buffered(1)),
            tall(HID),
            tall(HID),
            tall(HID),
            tall(SLOTS),
            tall(SLOTS),
            tall(1),
            pl.BlockSpec((1, 1, TILE), lambda i: (i, 0, 0)),
        ],
        out_specs=[tall(HID), tall(HID), tall(1)],
        out_shape=[
            jax.ShapeDtypeStruct((ROWS, HID), BF),
            jax.ShapeDtypeStruct((ROWS, HID), BF),
            jax.ShapeDtypeStruct((ROWS, 1), F32),
        ],
        compiler_params=pltpu.CompilerParams(vmem_limit_bytes=40 * MIB),
        cost_estimate=pl.CostEstimate(flops=3 * ROWS * D * HID, bytes_accessed=14 * MIB, transcendentals=ROWS * HID),
        name="backward",
    )(both, w_down, gate, up, hidden, xx, yy, ids.reshape(ROWS, 1), ids.reshape(steps, 1, TILE))


def grads_kernel(x_ref, y_ref, hidden_ref, dg_ref, du_ref, factor_ref, gg_ref, gu_ref, gd_ref, scaled, turned):
    @pl.when(pl.program_id(0) == 0)
    def _():
        factor = factor_ref[...]
        scaled[:, :HID] = (factor * dg_ref[...].astype(F32)).astype(BF)
        scaled[:, HID:] = (factor * du_ref[...].astype(F32)).astype(BF)
        turned[...] = hidden_ref[...].T

    x = x_ref[...].reshape(ROWS, COLS)
    both = dot(x, scaled[...], ((0,), (0,))).astype(BF)
    gg_ref[0] = both[:, :HID]
    gu_ref[0] = both[:, HID:]
    cot = (factor_ref[...] * y_ref[...].reshape(ROWS, COLS).astype(F32)).astype(BF)
    gd_ref[0] = dot(turned[...], cot, ((1,), (0,))).astype(BF)


def gradients(both, hidden, d_gate, d_up, factor):
    def whole(a):
        return pl.BlockSpec(a.shape, lambda i: (0, 0), pipeline_mode=pl.Buffered(1))

    return pl.pallas_call(
        grads_kernel,
        grid=(D // COLS,),
        in_specs=[
            pl.BlockSpec((BLOCKS, SLOTS, COLS), lambda i: (0, 0, i)),
            pl.BlockSpec((BLOCKS, SLOTS, COLS), lambda i: (0, 1, i)),
            whole(hidden),
            whole(d_gate),
            whole(d_up),
            whole(factor),
        ],
        out_specs=[
            pl.BlockSpec((1, COLS, HID), lambda i: (0, i, 0)),
            pl.BlockSpec((1, COLS, HID), lambda i: (0, i, 0)),
            pl.BlockSpec((1, HID, COLS), lambda i: (0, 0, i)),
        ],
        out_shape=[
            jax.ShapeDtypeStruct((1, D, HID), BF),
            jax.ShapeDtypeStruct((1, D, HID), BF),
            jax.ShapeDtypeStruct((1, HID, D), BF),
        ],
        scratch_shapes=[pltpu.VMEM((ROWS, 2 * HID), BF), pltpu.VMEM((HID, ROWS), BF)],
        compiler_params=pltpu.CompilerParams(vmem_limit_bytes=40 * MIB),
        cost_estimate=pl.CostEstimate(flops=6 * ROWS * D * HID, bytes_accessed=18 * MIB, transcendentals=0),
        name="gradients",
    )(both, both, hidden, d_gate, d_up, factor)


def on_device(tokens, cotangent, routes, example_ids, w_gate, w_up, w_down):
    ix, iz = lax.axis_index("x"), lax.axis_index("z")
    my_row = ix * NZ + iz
    tok_count, width = tokens.shape
    radius = math.sqrt(3.0 * D * FF * NE / (BLOCKS * EX_ROW))
    flat_routes = routes.reshape(-1)
    owner_hot = (flat_routes[:, None] == jnp.arange(NE)[None, :]).astype(jnp.int32)
    before = jnp.cumsum(owner_hot, axis=0) - owner_hot
    slot_of = flat_routes * CAP + jnp.sum(before * owner_hot, axis=1)
    placed = (jnp.arange(SLOTS)[:, None] == slot_of[None, :]).astype(jnp.int32)
    placed = jnp.sum(placed.reshape(SLOTS, tok_count, 2), axis=2)
    placed_bf = placed.astype(BF)
    filled = jnp.sum(placed, axis=1) > 0
    send_ids = jnp.where(filled, jnp.sum(placed * example_ids.reshape(-1)[None, :], axis=1), -1)
    send_x = jnp.dot(placed_bf, tokens, preferred_element_type=F32).astype(BF)
    send_dy = jnp.dot(placed_bf, cotangent, preferred_element_type=F32).astype(BF)
    id_cols = jnp.broadcast_to(send_ids.astype(BF)[:, None], (SLOTS, 128))
    send = jnp.concatenate(
        [
            jnp.concatenate([send_x, id_cols], axis=1).reshape(NE, CAP, width + 128),
            jnp.concatenate([send_dy, id_cols], axis=1).reshape(NE, CAP, width + 128),
        ],
        axis=1,
    )
    got = lax.all_to_all(send, EXPERT, split_axis=0, concat_axis=0, tiled=True)
    local_x = got[:, :CAP, :width].reshape(SLOTS, width)
    local_dy = got[:, CAP:, :width].reshape(SLOTS, width)
    local_ids = got[:, :CAP, width].reshape(SLOTS, 1).astype(F32)
    both = lax.all_gather(jnp.concatenate([local_x, local_dy], axis=0), ("x", "z"), axis=0)
    last = ((1,), (1,))
    notes = jnp.concatenate(
        [dot(local_x, local_x, last), dot(local_dy, local_dy, last), jnp.broadcast_to(local_ids, (SLOTS, 64))], axis=1
    )
    notes = spread(notes, ("x", "z"), BLOCKS).reshape(BLOCKS, SLOTS, 128)
    xx = notes[:, :, :SLOTS].reshape(ROWS, SLOTS)
    yy = notes[:, :, SLOTS : 2 * SLOTS].reshape(ROWS, SLOTS)
    ids = notes[:, :, 2 * SLOTS]
    gate, up, hidden, left, right = forward(both, w_gate, w_up, w_down, D // 2)
    own_out = jnp.concatenate([sum_z_x(left, ix, iz), sum_x_z(right, ix, iz)], axis=1)
    returned = lax.all_to_all(own_out.reshape(NE, CAP, width), EXPERT, split_axis=0, concat_axis=0, tiled=True)
    mixed = jnp.dot(placed_bf.T, returned.reshape(SLOTS, width), preferred_element_type=F32).astype(BF)
    d_gate, d_up, row_sums = backward(both, w_down, gate, up, hidden, xx, yy, ids)
    ex_hot = (ids[:, :, None] == jnp.arange(EX_ROW, dtype=F32)[None, None, :]).astype(F32)
    partial_value = jnp.sum(ex_hot * row_sums.reshape(BLOCKS, SLOTS, 1), axis=1)
    squares = jnp.sum(spread(partial_value, ("x", "z"), BLOCKS).reshape(BLOCKS, BLOCKS, EX_ROW), axis=0)
    squares = jnp.sum(spread(squares, EXPERT, NE).reshape(NE, BLOCKS, EX_ROW), axis=0)
    norms_all = jnp.sqrt(squares)
    factors = radius / (norms_all + GAMMA)
    own_norms = lax.dynamic_slice_in_dim(norms_all, my_row, 1, 0)
    row_factor = jnp.sum(ex_hot * factors[:, None, :], axis=2).reshape(ROWS, 1)
    grad_gate, grad_up, grad_down = gradients(both, hidden, d_gate, d_up, row_factor)
    return (mixed, own_norms, grad_gate, grad_up, grad_down)


def solution(mesh):
    mesh = Mesh(mesh.devices.reshape(NX, NZ, 4, 2), ("x", "z", "y", "c"))
    data, every = ("x", "z"), ("x", "z", "y", "c")
    return jax.shard_map(
        on_device,
        mesh=mesh,
        in_specs=(
            P(every, None),
            P(every, None),
            P(every, None),
            P(data, EXPERT),
            P(EXPERT, None, data),
            P(EXPERT, None, data),
            P(EXPERT, data, None),
        ),
        out_specs=(
            P(every, None),
            P(data, None),
            P(EXPERT, None, data),
            P(EXPERT, None, data),
            P(EXPERT, data, None),
        ),
        check_vma=False,
    )
```

time: 470 us -> 300 us (0.64)
  waiting for transfers between devices: 264 us -> 146 us
  blocking collectives: 113 us -> 14 us
  matrix products: 52.5 us -> 2.51 us
  starting transfers between devices: 14.4 us -> 56.5 us
  Pallas kernels: 0 us -> 24.5 us
  local copies, waits for them, and re-layouts: 7.09 us -> 23.1 us
  other arithmetic: 3.24 us -> 17.8 us
    reduce_scatter x1 -> x0, waiting for transfers between devices: 103 us -> none  [on_device(): lax.psum_scatter(jnp.dot(hidden, w_down[0], preferred_element_type=jnp.fl...]
    psum x1 -> x0, blocking collectives: 78.8 us -> none  [on_device(): squares = lax.psum(partial_value, ('dp', 'expert'))]
    all_gather x2 -> x1, waiting for transfers between devices: 157 us -> 92.9 us  [on_device(): lax.all_gather(jnp.concatenate([local_x, local_dy], axis=0), ('x', 'z'),...]
    dot_general x15 -> x5, matrix products: 52.5 us -> 2.51 us  [the longest x1 1.13 us: on_device(): jnp.dot(placed_bf, cotangent, preferred_element_type=F32).astype(BF)]
    ppermute x0 -> x22, waiting for transfers between devices: none -> 33.3 us  [shift(): return lax.ppermute(a, axis, [(i, (i + step) % n) for i in range(n)])]
    ppermute x0 -> x22, starting transfers between devices: none -> 25.3 us  [shift(): return lax.ppermute(a, axis, [(i, (i + step) % n) for i in range(n)])]
    pallas_call x0 -> x3, Pallas kernels: none -> 24.5 us  [the longest x1 10.5 us: gradients(): pl.pallas_call(grads_kernel, grid=(D // COLS,), in_specs=[pl.BlockSpec((B...]
    all_to_all x2 -> x4, starting transfers between devices: 14.3 us -> 31.2 us  [the longest x3 23.2 us: spread(): lax.all_to_all(jnp.broadcast_to(a[None], (n,) + a.shape), axes, 0, 0, til...]
  transfers between devices with their start and end apart: 5 -> 27, of which waited for: 4 -> 11; matrix products, arithmetic and copies ran while one was open for 9% -> 8% of each run, Pallas kernels for 0% -> 4%
where the time goes in v1:
time: 300 us; the launch traced here: 299 us
  waiting for transfers between devices  146 us (49%)
  starting transfers between devices  56.5 us (19%)
  Pallas kernels  24.5 us (8%)
  local copies, waits for them, and re-layouts  23.1 us (8%)
  other arithmetic  17.8 us (6%)
  between operations  14.7 us (5%)
  blocking collectives  14 us (5%)
    all_gather x1, waiting for transfers between devices, on_device(): lax.all_gather(jnp.concatenate([local_x, local_dy], axis=0), ('x', 'z'),...  92.9 us
    ppermute x22, waiting for transfers between devices, shift(): return lax.ppermute(a, axis, [(i, (i + step) % n) for i in range(n)])  33.3 us
    ppermute x22, starting transfers between devices, shift(): return lax.ppermute(a, axis, [(i, (i + step) % n) for i in range(n)])  25.3 us
    all_to_all x3, starting transfers between devices, spread(): lax.all_to_all(jnp.broadcast_to(a[None], (n,) + a.shape), axes, 0, 0, til...  23.2 us
    all_to_all x3, waiting for transfers between devices, spread(): lax.all_to_all(jnp.broadcast_to(a[None], (n,) + a.shape), axes, 0, 0, til...  19.8 us
    all_to_all x1, blocking collectives, on_device(): got = lax.all_to_all(send, EXPERT, split_axis=0, concat_axis=0, tiled=True)  14 us
    unnamed x47, local copies, waits for them, and re-layouts  12.5 us
    pallas_call x1, Pallas kernels, gradients(): pl.pallas_call(grads_kernel, grid=(D // COLS,), in_specs=[pl.BlockSpec((B...  10.5 us
  transfers between devices with their start and end apart: 27, of which 11 were waited for; matrix products, arithmetic and copies ran while one was open for 8% of the time, Pallas kernels for 4%

profile of v1, /device:TPU:1, one launch (start us, length us, event | category | flops | bytes accessed | tf_op | source)
XLA Modules:
  0.0 299.2 jit_solution(10894330795111850190)
XLA Ops:
  7.2 0.8 copy.65
  8.6 0.7 multiply_add_fusion
  9.5 0.7 multiply_reduce_fusion
  10.4 1.1 convolution_convert_fusion
  12.0 14.0 %all_to_all.25 = bf16[8,8,3200]{2,1,0:T(8,128)(2,1)S(1)} all-to-all(bf16[8,8,3200]{2,1,0:T(8,128)(2,1)S(1)} %pad_maximum_fusion.2), channel_id=1, replica_groups=mesh['x'=4,'z'=8,'y'=4,'c'=2] {'y','c'}, dimensions={0} | all-to-all | bytes 819200 | tf_op jit(solution)/shard_map/all_to_all | solution.py:243
  26.3 0.8 pad_maximum_fusion.3
  27.8 0.9 broadcast_in_dim.17
  28.6 11.0 %all-to-all-start.2 = ((f32[32,32,128]{2,1,0:T(8,128)}), f32[32,32,128]{2,1,0:T(8,128)S(1)}, u32[]{:S(2)}, u32[]{:S(2)}) async-start(f32[32,32,128]{2,1,0:T(8,128)} %broadcast_in_dim.17), calls=%async_computation.2 | async-start | bytes 1048576 | tf_op jit(solution)/shard_map/all_to_all | solution.py:76
  39.9 15.8 %all-to-all-done.2 = f32[32,32,128]{2,1,0:T(8,128)S(1)} async-done(((f32[32,32,128]{2,1,0:T(8,128)}), f32[32,32,128]{2,1,0:T(8,128)S(1)}, u32[]{:S(2)}, u32[]{:S(2)}) %all-to-all-start.2) | async-done | bytes 524320 | tf_op jit(solution)/shard_map/all_to_all | solution.py:76
  55.8 0.8 copy-done.15
  57.1 1.6 fusion.7
  58.7 92.9 %all-gather.3.cloned.1.call-done = bf16[2048,3072]{1,0:T(8,128)(2,1)} async-done(((bf16[64,3072]{1,0:T(8,128)(2,1)}), bf16[2048,3072]{1,0:T(8,128)(2,1)}) %all-gather.3.cloned.1.call-update) | async-done | bytes 12582928 | tf_op jit(solution)/shard_map/all_gather | solution.py:247
  151.6 1.4 copy-done.13
  153.0 1.4 copy-done.14
  154.4 7.4 %forward.1 = (f32[1024,256]{1,0:T(8,128)S(1)}, f32[1024,256]{1,0:T(8,128)S(1)}, bf16[1024,256]{1,0:T(8,128)(2,1)S(1)}, bf16[1024,1536]{1,0:T(8,128)(2,1)S(1)}, bf16[1024,1536]{1,0:T(8,128)(2,1)S(1)}) custom-call(bf16[32,64,3072]{2,1,0:T(8,128)(2,1)} %bitcast.40, bf16[1,3072,256]{2,1,0:T(8,128)(2,1)S(1)} %copy-done.13, bf16[1,3072,256]{2,1,0:T(8,128)(2,1)S(1)} %copy-done.14, ...), custom_call_target="tpu_custom_call" | custom-call | flops 4831838208 | bytes 20971520 | tf_op jit(solution)/shard_map/forward/pallas_call | solution.py:103
  161.8 1.6 copy-done.1
  163.4 1.6 copy-done.3
  165.1 6.7 %backward.1 = (bf16[1024,256]{1,0:T(8,128)(2,1)S(1)}, bf16[1024,256]{1,0:T(8,128)(2,1)S(1)}, f32[1024,1]{1,0:T(8,128)S(1)}) custom-call(bf16[32,64,3072]{2,1,0:T(8,128)(2,1)} %bitcast.41, bf16[1,256,3072]{2,1,0:T(8,128)(2,1)S(1)} %copy-done.7, f32[1024,256]{1,0:T(8,128)S(1)} %get-tuple-element.18.gate_ref, f32[1024,256]{1,0:T(8,128)S(1)} %get-tuple-element.19.up_ref, ...), custom_call_target="tpu_custom_call" | custom-call | flops 2415919104 | bytes 14680064 | tf_op jit(solution)/shard_map/backward/pallas_call | solution.py:145
  171.8 0.8 copy-done.8
  172.6 0.8 copy-done.9
  173.4 0.8 copy-done.11
  174.2 1.2 reduce.2
  175.6 0.7 reshape.105
  176.4 5.3 %all-to-all-start.3 = ((f32[32,1,192]{2,1,0:T(1,128)}), f32[32,1,192]{2,1,0:T(1,128)S(1)}, u32[]{:S(2)}, u32[]{:S(2)}) async-start(f32[32,1,192]{2,1,0:T(1,128)} %reshape.105), calls=%async_computation.3 | async-start | bytes 65536 | tf_op jit(solution)/shard_map/all_to_all | solution.py:76
  181.7 2.1 constant_dynamic-slice_fusion.3
  183.8 1.2 collective-permute-start
  185.0 1.4 collective-permute-start.4
  186.4 4.0 %all-to-all-done.3 = f32[32,1,192]{2,1,0:T(1,128)S(1)} async-done(((f32[32,1,192]{2,1,0:T(1,128)}), f32[32,1,192]{2,1,0:T(1,128)S(1)}, u32[]{:S(2)}, u32[]{:S(2)}) %all-to-all-start.3) | async-done | bytes 24608 | tf_op jit(solution)/shard_map/all_to_all | solution.py:76
  191.0 0.7 reduce.4
  191.8 0.7 reshape.107
  192.5 6.9 %all-to-all-start.4 = ((f32[8,1,192]{2,1,0:T(1,128)}), f32[8,1,192]{2,1,0:T(1,128)S(1)}, u32[]{:S(2)}, u32[]{:S(2)}) async-start(f32[8,1,192]{2,1,0:T(1,128)} %reshape.107), calls=%async_computation.4 | async-start | bytes 16384 | tf_op jit(solution)/shard_map/all_to_all | solution.py:76
  199.4 2.7 constant_dynamic-slice_fusion
  202.3 2.4 collective-permute-start.13
  204.7 0.7 reduce.5
  205.5 1.1 add_convert_fusion.9
  206.7 1.0 pad_maximum_fusion.4
  208.1 2.4 collective-permute-start.5
  210.5 3.8 %collective-permute-done.11 = bf16[1,8,16,1536]{3,2,1,0:T(8,128)(2,1)} collective-permute-done((bf16[1,8,16,1536]{3,2,1,0:T(8,128)(2,1)}, bf16[1,8,16,1536]{3,2,1,0:T(8,128)(2,1)}, u32[]{:S(2)}, u32[]{:S(2)}) %collective-permute-start.11) | collective-permute-done | bytes 393248 | tf_op jit(solution)/shard_map/ppermute | solution.py:32
  214.3 1.6 add_convert_fusion.2
  215.9 0.9 pad_maximum_fusion.1
  216.9 2.3 collective-permute-start.14
  219.2 1.1 add_convert_fusion.7
  220.6 2.4 collective-permute-start.6
  223.0 0.9 pad_maximum_fusion
  224.1 1.4 reshape.102.factor_ref
  225.4 5.6 %collective-permute-done.2 = bf16[4,1,32,1536]{3,2,1,0:T(8,128)(2,1)} collective-permute-done((bf16[4,1,32,1536]{3,2,1,0:T(8,128)(2,1)}, bf16[4,1,32,1536]{3,2,1,0:T(8,128)(2,1)}, u32[]{:S(2)}, u32[]{:S(2)}) %collective-permute-start.2) | collective-permute-done | bytes 393248 | tf_op jit(solution)/shard_map/ppermute | solution.py:32
  231.0 1.3 add_convert_fusion.6
  232.4 2.5 collective-permute-start.7
  235.5 7.1 %collective-permute-done.12 = bf16[1,8,32,1536]{3,2,1,0:T(8,128)(2,1)} collective-permute-done((bf16[1,8,32,1536]{3,2,1,0:T(8,128)(2,1)}, bf16[1,8,32,1536]{3,2,1,0:T(8,128)(2,1)}, u32[]{:S(2)}, u32[]{:S(2)}) %collective-permute-start.12) | collective-permute-done | bytes 786464 | tf_op jit(solution)/shard_map/ppermute | solution.py:32
  242.5 1.9 add_convert_fusion
  244.5 0.7 collective-permute-start.21
  245.3 2.0 collective-permute-start.19
  247.3 3.6 %collective-permute-start.18 = (bf16[1,1,32,1536]{3,2,1,0:T(8,128)(2,1)S(1)}, bf16[1,1,32,1536]{3,2,1,0:T(8,128)(2,1)S(1)}, u32[]{:S(2)}, u32[]{:S(2)}) collective-permute-start(bf16[1,1,32,1536]{3,2,1,0:T(8,128)(2,1)S(1)} %get-tuple-element.64), channel_id=1, source_target_pairs={{0,32},{8,40},{16,48},{24,56},{32,0},{40,8},{48,16},{56,24},{1,33}... | collective-permute-start | bytes 294920 | tf_op jit(solution)/shard_map/ppermute | solution.py:32
  251.6 1.5 collective-permute-start.16
  253.1 0.9 collective-permute-start.15
  254.0 3.2 %collective-permute-done.19 = bf16[1,1,32,1536]{3,2,1,0:T(8,128)(2,1)S(1)} collective-permute-done((bf16[1,1,32,1536]{3,2,1,0:T(8,128)(2,1)S(1)}, bf16[1,1,32,1536]{3,2,1,0:T(8,128)(2,1)S(1)}, u32[]{:S(2)}, u32[]{:S(2)}) %collective-permute-start.19) | collective-permute-done | bytes 98336 | tf_op jit(solution)/shard_map/ppermute | solution.py:32
  257.5 3.3 %collective-permute-done.17 = bf16[1,1,32,1536]{3,2,1,0:T(8,128)(2,1)S(1)} collective-permute-done((bf16[1,1,32,1536]{3,2,1,0:T(8,128)(2,1)S(1)}, bf16[1,1,32,1536]{3,2,1,0:T(8,128)(2,1)S(1)}, u32[]{:S(2)}, u32[]{:S(2)}) %collective-permute-start.17) | collective-permute-done | bytes 98336 | tf_op jit(solution)/shard_map/ppermute | solution.py:32
  260.9 2.4 collective-permute-done.16
  263.3 7.2 %collective-permute-done.15 = bf16[1,1,32,1536]{3,2,1,0:T(8,128)(2,1)S(1)} collective-permute-done((bf16[1,1,32,1536]{3,2,1,0:T(8,128)(2,1)S(1)}, bf16[1,1,32,1536]{3,2,1,0:T(8,128)(2,1)S(1)}, u32[]{:S(2)}, u32[]{:S(2)}) %collective-permute-start.15) | collective-permute-done | bytes 98336 | tf_op jit(solution)/shard_map/ppermute | solution.py:32
  270.6 1.0 add_convert_fusion.11
  271.6 0.8 pad_maximum_fusion.8
  272.4 7.9 %all-to-all-start.1 = ((bf16[8,4,3072]{2,1,0:T(4,128)(2,1)}), bf16[8,4,3072]{2,1,0:T(4,128)(2,1)S(1)}, u32[]{:S(2)}, u32[]{:S(2)}) async-start(bf16[8,4,3072]{2,1,0:T(4,128)(2,1)} %pad_maximum_fusion.8), calls=%async_computation.1 | async-start | bytes 393216 | tf_op jit(solution)/shard_map/all_to_all | solution.py:258
  280.3 10.5 %gradients.1 = (bf16[1,3072,256]{2,1,0:T(8,128)(2,1)}, bf16[1,3072,256]{2,1,0:T(8,128)(2,1)}, bf16[1,256,3072]{2,1,0:T(8,128)(2,1)}) custom-call(bf16[32,64,3072]{2,1,0:T(8,128)(2,1)} %bitcast.42, bf16[32,64,3072]{2,1,0:T(8,128)(2,1)} %bitcast.43, bf16[1024,256]{1,0:T(8,128)(2,1)S(1)} %copy-done.5, bf16[1024,256]{1,0:T(8,128)(2,1)S(1)} %copy-done.10, ...), custom_call_target="tpu_custom_call" | custom-call | flops 4831838208 | bytes 18874368 | tf_op jit(solution)/shard_map/gradients/pallas_call | solution.py:191
  291.6 0.8 convolution_convert_fusion.2
  (107 shorter events, 7.7 us)
Async XLA Ops:
  7.2 3.0 %copy-start = (bf16[12,3072]{1,0:T(8,128)(2,1)S(1)}, bf16[12,3072]{1,0:T(8,128)(2,1)}, u32[]{:S(2)}) copy-start(bf16[12,3072]{1,0:T(8,128)(2,1)} %param.7) | copy-start | bytes 221188
  7.2 144.4 %all-gather.3.cloned.1.call-start = ((), (), s32[]{:S(2)}) async-start(), calls=%async_computation.5 | async-start | bytes 12976128 | tf_op jit(solution)/shard_map/all_gather | solution.py:247
  28.6 27.1 %all-to-all-start.2 = ((f32[32,32,128]{2,1,0:T(8,128)}), f32[32,32,128]{2,1,0:T(8,128)S(1)}, u32[]{:S(2)}, u32[]{:S(2)}) async-start(f32[32,32,128]{2,1,0:T(8,128)} %broadcast_in_dim.17), calls=%async_computation.2 | async-start | bytes 1048576 | tf_op jit(solution)/shard_map/all_to_all | solution.py:76
  55.8 0.8 copy-start.15
  56.8 94.8 %copy-start.7 = (bf16[1,256,3072]{2,1,0:T(8,128)(2,1)S(1)}, bf16[1,256,3072]{2,1,0:T(8,128)(2,1)}, u32[]{:S(2)}) copy-start(bf16[1,256,3072]{2,1,0:T(8,128)(2,1)} %wd_ref.3) | copy-start | bytes 4718596
  151.6 1.4 copy-start.13
  153.0 1.4 copy-start.14
  161.8 1.7 copy-start.1
  163.4 1.6 copy-start.3
  165.1 6.7 %copy-start.4 = (bf16[1024,256]{1,0:T(8,128)(2,1)}, bf16[1024,256]{1,0:T(8,128)(2,1)S(1)}, u32[]{:S(2)}) copy-start(bf16[1024,256]{1,0:T(8,128)(2,1)S(1)} %get-tuple-element.20.hidden_ref) | copy-start | bytes 1572868
  171.8 0.8 copy-start.8
  172.6 0.8 copy-start.9
  173.4 0.8 copy-start.11
  176.4 14.1 %all-to-all-start.3 = ((f32[32,1,192]{2,1,0:T(1,128)}), f32[32,1,192]{2,1,0:T(1,128)S(1)}, u32[]{:S(2)}, u32[]{:S(2)}) async-start(f32[32,1,192]{2,1,0:T(1,128)} %reshape.105), calls=%async_computation.3 | async-start | bytes 65536 | tf_op jit(solution)/shard_map/all_to_all | solution.py:76
  183.8 21.7 %collective-permute-start = (bf16[4,1,16,1536]{3,2,1,0:T(8,128)(2,1)}, bf16[4,1,16,1536]{3,2,1,0:T(8,128)(2,1)}, u32[]{:S(2)}, u32[]{:S(2)}) collective-permute-start(bf16[4,1,16,1536]{3,2,1,0:T(8,128)(2,1)} %get-tuple-element.50), channel_id=1, source_target_pairs={{0,8},{8,16},{16,24},{24,32},{32,40},{40,48},{48,56},{56,0},{1,9},... | collective-permute-start | bytes 589832 | tf_op jit(solution)/shard_map/ppermute | solution.py:32
  185.0 20.5 %collective-permute-start.4 = (bf16[4,1,16,1536]{3,2,1,0:T(8,128)(2,1)}, bf16[4,1,16,1536]{3,2,1,0:T(8,128)(2,1)}, u32[]{:S(2)}, u32[]{:S(2)}) collective-permute-start(bf16[4,1,16,1536]{3,2,1,0:T(8,128)(2,1)} %get-tuple-element.53), channel_id=1, source_target_pairs={{0,56},{8,0},{16,8},{24,16},{32,24},{40,32},{48,40},{56,48},{1,57}... | collective-permute-start | bytes 589832 | tf_op jit(solution)/shard_map/ppermute | solution.py:32
  192.5 12.2 %all-to-all-start.4 = ((f32[8,1,192]{2,1,0:T(1,128)}), f32[8,1,192]{2,1,0:T(1,128)S(1)}, u32[]{:S(2)}, u32[]{:S(2)}) async-start(f32[8,1,192]{2,1,0:T(1,128)} %reshape.107), calls=%async_computation.4 | async-start | bytes 16384 | tf_op jit(solution)/shard_map/all_to_all | solution.py:76
  199.4 6.1 %copy-start.2 = (bf16[1024,1536]{1,0:T(8,128)(2,1)S(1)}, bf16[1024,1536]{1,0:T(8,128)(2,1)}, u32[]{:S(2)}) copy-start(bf16[1024,1536]{1,0:T(8,128)(2,1)} %copy-done.1) | copy-start | bytes 9437188
  202.1 12.3 %collective-permute-start.11 = (bf16[1,8,16,1536]{3,2,1,0:T(8,128)(2,1)}, bf16[1,8,16,1536]{3,2,1,0:T(8,128)(2,1)}, u32[]{:S(2)}, u32[]{:S(2)}) collective-permute-start(bf16[1,8,16,1536]{3,2,1,0:T(8,128)(2,1)} %get-tuple-element.56), channel_id=1, source_target_pairs={{0,64},{64,128},{128,192},{192,0},{1,65},{65,129},{129,193},{193,1... | collective-permute-start | bytes 1179656 | tf_op jit(solution)/shard_map/ppermute | solution.py:32
  202.3 12.0 %collective-permute-start.13 = (bf16[1,8,16,1536]{3,2,1,0:T(8,128)(2,1)}, bf16[1,8,16,1536]{3,2,1,0:T(8,128)(2,1)}, u32[]{:S(2)}, u32[]{:S(2)}) collective-permute-start(bf16[1,8,16,1536]{3,2,1,0:T(8,128)(2,1)} %get-tuple-element.59), channel_id=1, source_target_pairs={{0,192},{64,0},{128,64},{192,128},{1,193},{65,1},{129,65},{193,129... | collective-permute-start | bytes 1179656 | tf_op jit(solution)/shard_map/ppermute | solution.py:32
  207.6 11.6 %collective-permute-start.1 = (bf16[4,1,32,1536]{3,2,1,0:T(8,128)(2,1)S(1)}, bf16[4,1,32,1536]{3,2,1,0:T(8,128)(2,1)S(1)}, u32[]{:S(2)}, u32[]{:S(2)}) collective-permute-start(bf16[4,1,32,1536]{3,2,1,0:T(8,128)(2,1)S(1)} %pad_maximum_fusion.4), channel_id=1, source_target_pairs={{0,8},{8,16},{16,24},{24,32},{32,40},{40,48},{48,56},{56,0},{1,9},... | collective-permute-start | bytes 1179656 | tf_op jit(solution)/shard_map/ppermute | solution.py:32
  208.0 7.9 %copy-start.18 = (bf16[1,8,16,1536]{3,2,1,0:T(8,128)(2,1)S(1)}, bf16[1,8,16,1536]{3,2,1,0:T(8,128)(2,1)}, u32[]{:S(2)}) copy-start(bf16[1,8,16,1536]{3,2,1,0:T(8,128)(2,1)} %get-tuple-element.57) | copy-start | bytes 1179652
  208.1 11.2 %collective-permute-start.5 = (bf16[4,1,32,1536]{3,2,1,0:T(8,128)(2,1)S(1)}, bf16[4,1,32,1536]{3,2,1,0:T(8,128)(2,1)S(1)}, u32[]{:S(2)}, u32[]{:S(2)}) collective-permute-start(bf16[4,1,32,1536]{3,2,1,0:T(8,128)(2,1)S(1)} %pad_maximum_fusion.5), channel_id=1, source_target_pairs={{0,56},{8,0},{16,8},{24,16},{32,24},{40,32},{48,40},{56,48},{1,57}... | collective-permute-start | bytes 1179656 | tf_op jit(solution)/shard_map/ppermute | solution.py:32
  216.9 6.1 %copy-start.17 = (bf16[1,8,16,1536]{3,2,1,0:T(8,128)(2,1)S(1)}, bf16[1,8,16,1536]{3,2,1,0:T(8,128)(2,1)}, u32[]{:S(2)}) copy-start(bf16[1,8,16,1536]{3,2,1,0:T(8,128)(2,1)} %get-tuple-element.58) | copy-start | bytes 1179652
  216.9 18.6 %collective-permute-start.14 = (bf16[1,8,32,1536]{3,2,1,0:T(8,128)(2,1)}, bf16[1,8,32,1536]{3,2,1,0:T(8,128)(2,1)}, u32[]{:S(2)}, u32[]{:S(2)}) collective-permute-start(bf16[1,8,32,1536]{3,2,1,0:T(8,128)(2,1)} %pad_maximum_fusion.1), channel_id=1, source_target_pairs={{0,192},{64,0},{128,64},{192,128},{1,193},{65,1},{129,65},{193,129... | collective-permute-start | bytes 2359304 | tf_op jit(solution)/shard_map/ppermute | solution.py:32
  220.3 10.7 %collective-permute-start.2 = (bf16[4,1,32,1536]{3,2,1,0:T(8,128)(2,1)}, bf16[4,1,32,1536]{3,2,1,0:T(8,128)(2,1)}, u32[]{:S(2)}, u32[]{:S(2)}) collective-permute-start(bf16[4,1,32,1536]{3,2,1,0:T(8,128)(2,1)} %get-tuple-element.46), channel_id=1, source_target_pairs={{0,8},{8,16},{16,24},{24,32},{32,40},{40,48},{48,56},{56,0},{1,9},... | collective-permute-start | bytes 1179656 | tf_op jit(solution)/shard_map/ppermute | solution.py:32
  220.6 10.4 %collective-permute-start.6 = (bf16[4,1,32,1536]{3,2,1,0:T(8,128)(2,1)}, bf16[4,1,32,1536]{3,2,1,0:T(8,128)(2,1)}, u32[]{:S(2)}, u32[]{:S(2)}) collective-permute-start(bf16[4,1,32,1536]{3,2,1,0:T(8,128)(2,1)} %get-tuple-element.47), channel_id=1, source_target_pairs={{0,56},{8,0},{16,8},{24,16},{32,24},{40,32},{48,40},{56,48},{1,57}... | collective-permute-start | bytes 1179656 | tf_op jit(solution)/shard_map/ppermute | solution.py:32
  223.9 18.6 %collective-permute-start.12 = (bf16[1,8,32,1536]{3,2,1,0:T(8,128)(2,1)}, bf16[1,8,32,1536]{3,2,1,0:T(8,128)(2,1)}, u32[]{:S(2)}, u32[]{:S(2)}) collective-permute-start(bf16[1,8,32,1536]{3,2,1,0:T(8,128)(2,1)} %pad_maximum_fusion), channel_id=1, source_target_pairs={{0,64},{64,128},{128,192},{192,0},{1,65},{65,129},{129,193},{193,1... | collective-permute-start | bytes 2359304 | tf_op jit(solution)/shard_map/ppermute | solution.py:32
  232.4 15.0 %collective-permute-start.7 = (bf16[4,1,32,1536]{3,2,1,0:T(8,128)(2,1)S(1)}, bf16[4,1,32,1536]{3,2,1,0:T(8,128)(2,1)S(1)}, u32[]{:S(2)}, u32[]{:S(2)}) collective-permute-start(bf16[4,1,32,1536]{3,2,1,0:T(8,128)(2,1)S(1)} %get-tuple-element.45), channel_id=1, source_target_pairs={{0,56},{8,0},{16,8},{24,16},{32,24},{40,32},{48,40},{56,48},{1,57}... | collective-permute-start | bytes 1179656 | tf_op jit(solution)/shard_map/ppermute | solution.py:32
  234.8 16.1 %collective-permute-start.3 = (bf16[4,1,32,1536]{3,2,1,0:T(8,128)(2,1)S(1)}, bf16[4,1,32,1536]{3,2,1,0:T(8,128)(2,1)S(1)}, u32[]{:S(2)}, u32[]{:S(2)}) collective-permute-start(bf16[4,1,32,1536]{3,2,1,0:T(8,128)(2,1)S(1)} %get-tuple-element.44), channel_id=1, source_target_pairs={{0,8},{8,16},{16,24},{24,32},{32,40},{40,48},{48,56},{56,0},{1,9},... | collective-permute-start | bytes 1179656 | tf_op jit(solution)/shard_map/ppermute | solution.py:32
  244.5 7.1 %collective-permute-start.21 = (bf16[1,1,32,1536]{3,2,1,0:T(8,128)(2,1)S(1)}, bf16[1,1,32,1536]{3,2,1,0:T(8,128)(2,1)S(1)}, u32[]{:S(2)}, u32[]{:S(2)}) collective-permute-start(bf16[1,1,32,1536]{3,2,1,0:T(8,128)(2,1)S(1)} %get-tuple-element.61), channel_id=1, source_target_pairs={{0,56},{8,0},{16,8},{24,16},{32,24},{40,32},{48,40},{56,48},{1,57}... | collective-permute-start | bytes 294920 | tf_op jit(solution)/shard_map/ppermute | solution.py:32
  245.2 7.8 %collective-permute-start.20 = (bf16[1,1,32,1536]{3,2,1,0:T(8,128)(2,1)S(1)}, bf16[1,1,32,1536]{3,2,1,0:T(8,128)(2,1)S(1)}, u32[]{:S(2)}, u32[]{:S(2)}) collective-permute-start(bf16[1,1,32,1536]{3,2,1,0:T(8,128)(2,1)S(1)} %get-tuple-element.62), channel_id=1, source_target_pairs={{0,48},{8,56},{16,0},{24,8},{32,16},{40,24},{48,32},{56,40},{1,49}... | collective-permute-start | bytes 294920 | tf_op jit(solution)/shard_map/ppermute | solution.py:32
  245.3 11.9 %collective-permute-start.19 = (bf16[1,1,32,1536]{3,2,1,0:T(8,128)(2,1)S(1)}, bf16[1,1,32,1536]{3,2,1,0:T(8,128)(2,1)S(1)}, u32[]{:S(2)}, u32[]{:S(2)}) collective-permute-start(bf16[1,1,32,1536]{3,2,1,0:T(8,128)(2,1)S(1)} %get-tuple-element.63), channel_id=1, source_target_pairs={{0,40},{8,48},{16,56},{24,0},{32,8},{40,16},{48,24},{56,32},{1,41}... | collective-permute-start | bytes 294920 | tf_op jit(solution)/shard_map/ppermute | solution.py:32
  247.3 9.9 %collective-permute-start.18 = (bf16[1,1,32,1536]{3,2,1,0:T(8,128)(2,1)S(1)}, bf16[1,1,32,1536]{3,2,1,0:T(8,128)(2,1)S(1)}, u32[]{:S(2)}, u32[]{:S(2)}) collective-permute-start(bf16[1,1,32,1536]{3,2,1,0:T(8,128)(2,1)S(1)} %get-tuple-element.64), channel_id=1, source_target_pairs={{0,32},{8,40},{16,48},{24,56},{32,0},{40,8},{48,16},{56,24},{1,33}... | collective-permute-start | bytes 294920 | tf_op jit(solution)/shard_map/ppermute | solution.py:32
  250.9 10.0 %collective-permute-start.17 = (bf16[1,1,32,1536]{3,2,1,0:T(8,128)(2,1)S(1)}, bf16[1,1,32,1536]{3,2,1,0:T(8,128)(2,1)S(1)}, u32[]{:S(2)}, u32[]{:S(2)}) collective-permute-start(bf16[1,1,32,1536]{3,2,1,0:T(8,128)(2,1)S(1)} %get-tuple-element.65), channel_id=1, source_target_pairs={{0,24},{8,32},{16,40},{24,48},{32,56},{40,0},{48,8},{56,16},{1,25}... | collective-permute-start | bytes 294920 | tf_op jit(solution)/shard_map/ppermute | solution.py:32
  251.6 2.4 copy-start.16
  251.6 11.7 %collective-permute-start.16 = (bf16[1,1,32,1536]{3,2,1,0:T(8,128)(2,1)S(1)}, bf16[1,1,32,1536]{3,2,1,0:T(8,128)(2,1)S(1)}, u32[]{:S(2)}, u32[]{:S(2)}) collective-permute-start(bf16[1,1,32,1536]{3,2,1,0:T(8,128)(2,1)S(1)} %get-tuple-element.66), channel_id=1, source_target_pairs={{0,16},{8,24},{16,32},{24,40},{32,48},{40,56},{48,0},{56,8},{1,17}... | collective-permute-start | bytes 294920 | tf_op jit(solution)/shard_map/ppermute | solution.py:32
  253.1 27.2 %copy-start.5 = (bf16[1024,256]{1,0:T(8,128)(2,1)S(1)}, bf16[1024,256]{1,0:T(8,128)(2,1)}, u32[]{:S(2)}) copy-start(bf16[1024,256]{1,0:T(8,128)(2,1)} %copy-done.4) | copy-start | bytes 1572868
  253.1 27.2 %copy-start.6 = (f32[1024,1]{1,0:T(8,128)S(1)}, f32[1024,1]{1,0:T(8,128)}, u32[]{:S(2)}) copy-start(f32[1024,1]{1,0:T(8,128)} %reshape.102.factor_ref) | copy-start | bytes 12292
  253.1 27.3 %copy-start.10 = (bf16[1024,256]{1,0:T(8,128)(2,1)S(1)}, bf16[1024,256]{1,0:T(8,128)(2,1)}, u32[]{:S(2)}) copy-start(bf16[1024,256]{1,0:T(8,128)(2,1)} %copy-done.9) | copy-start | bytes 1572868
  253.1 27.3 %copy-start.12 = (bf16[1024,256]{1,0:T(8,128)(2,1)S(1)}, bf16[1024,256]{1,0:T(8,128)(2,1)}, u32[]{:S(2)}) copy-start(bf16[1024,256]{1,0:T(8,128)(2,1)} %copy-done.11) | copy-start | bytes 1572868
  253.1 17.4 %collective-permute-start.15 = (bf16[1,1,32,1536]{3,2,1,0:T(8,128)(2,1)S(1)}, bf16[1,1,32,1536]{3,2,1,0:T(8,128)(2,1)S(1)}, u32[]{:S(2)}, u32[]{:S(2)}) collective-permute-start(bf16[1,1,32,1536]{3,2,1,0:T(8,128)(2,1)S(1)} %get-tuple-element.60), channel_id=1, source_target_pairs={{0,8},{8,16},{16,24},{24,32},{32,40},{40,48},{48,56},{56,0},{1,9},... | collective-permute-start | bytes 294920 | tf_op jit(solution)/shard_map/ppermute | solution.py:32
  257.2 13.4 %collective-permute-start.10 = (bf16[1,1,32,1536]{3,2,1,0:T(8,128)(2,1)S(1)}, bf16[1,1,32,1536]{3,2,1,0:T(8,128)(2,1)S(1)}, u32[]{:S(2)}, u32[]{:S(2)}) collective-permute-start(bf16[1,1,32,1536]{3,2,1,0:T(8,128)(2,1)S(1)} %get-tuple-element.72), channel_id=1, source_target_pairs={{0,192},{64,0},{128,64},{192,128},{1,193},{65,1},{129,65},{193,129... | collective-permute-start | bytes 294920 | tf_op jit(solution)/shard_map/ppermute | solution.py:32
  257.2 13.4 %collective-permute-start.9 = (bf16[1,1,32,1536]{3,2,1,0:T(8,128)(2,1)S(1)}, bf16[1,1,32,1536]{3,2,1,0:T(8,128)(2,1)S(1)}, u32[]{:S(2)}, u32[]{:S(2)}) collective-permute-start(bf16[1,1,32,1536]{3,2,1,0:T(8,128)(2,1)S(1)} %get-tuple-element.73), channel_id=1, source_target_pairs={{0,128},{64,192},{128,0},{192,64},{1,129},{65,193},{129,1},{193,65... | collective-permute-start | bytes 294920 | tf_op jit(solution)/shard_map/ppermute | solution.py:32
  260.9 9.7 %collective-permute-start.8 = (bf16[1,1,32,1536]{3,2,1,0:T(8,128)(2,1)S(1)}, bf16[1,1,32,1536]{3,2,1,0:T(8,128)(2,1)S(1)}, u32[]{:S(2)}, u32[]{:S(2)}) collective-permute-start(bf16[1,1,32,1536]{3,2,1,0:T(8,128)(2,1)S(1)} %get-tuple-element.71), channel_id=1, source_target_pairs={{0,64},{64,128},{128,192},{192,0},{1,65},{65,129},{129,193},{193,1... | collective-permute-start | bytes 294920 | tf_op jit(solution)/shard_map/ppermute | solution.py:32
  272.4 19.1 %all-to-all-start.1 = ((bf16[8,4,3072]{2,1,0:T(4,128)(2,1)}), bf16[8,4,3072]{2,1,0:T(4,128)(2,1)S(1)}, u32[]{:S(2)}, u32[]{:S(2)}) async-start(bf16[8,4,3072]{2,1,0:T(4,128)(2,1)} %pad_maximum_fusion.8), calls=%async_computation.1 | async-start | bytes 393216 | tf_op jit(solution)/shard_map/all_to_all | solution.py:258
Sparse Core Ops, SparseCore 0:
  27.2 124.3 all-gather.2
